TPU v7x, 32 devices: a whole 2x2x4 slice. The times are simulated.
32 devices in a mesh: dp: 8 (over z, x), bin: 4 (over y, core).
Axes of the slice: x: 2, y: 2, z: 4, core: 2. Of those that a mesh axis runs over, the one named last changes fastest.
Arguments:
- features: bfloat16 [4096, 2, 2048], P(('dp', 'bin')), may hold values from -90 to 90
- head_weight: bfloat16 [2048, 1024], P('bin'), may hold values from -9 to 9
- bin_of_row: int32 [4096, 1], P(('dp', 'bin')), may hold values from 0 to 11; in each aligned block of 128 rows (0 to 127, 128 to 255, ...) at most 21 rows name the same one
- bin_owner: int32 [12], replicated, may hold values from 0 to 7, never falling along the last dimension, each value on 1 to 2 neighbouring positions
- bin_link: int32 [12], replicated, may hold values 0 or 1
Outputs:
- grad_rows: bfloat16 [4096, 2, 1024], P(('dp', 'bin'))
- grad_weight: float32 [2048, 1024], P(('bin', 'dp'))
Inputs may be any that keep to these rules, and one draw needn't show every extreme that they name: `bin_of_row`: in the rows of one device no bin appears more than 21 times. `bin_owner`: never falls; every owner holds 1 to 2 consecutive bins.
All inputs are finite; a program needn't handle non-finite values.
Results may differ from a plain program's by a relative error of at most 0.012.
Values may be sent and summed in bfloat16 or wider, within the bound.
A program may use at most 64 MiB of HBM per device.

v0:
```python
import functools

import jax
import jax.numpy as jnp
from jax import lax
from jax.experimental import pallas as pl
from jax.experimental.pallas import tpu as pltpu
from jax.sharding import PartitionSpec as P

MOSTB = 2


SOFTMAX_TEMP_SCALE = 0.1


def allowed_mask(valid, first, bin_link, group_slots, per_bin):
    per_owner = per_bin * MOSTB
    position = jnp.arange(group_slots, dtype=jnp.int32)
    local_bin = position % per_owner // per_bin
    padded = jnp.concatenate([bin_link, jnp.zeros((MOSTB,), jnp.int32)])
    nearby = lax.dynamic_slice(padded, (first,), (MOSTB,))
    lower = jnp.minimum(local_bin[:, None], local_bin[None, :])
    linked = jnp.zeros((group_slots, group_slots), jnp.int32)
    for height in range(MOSTB):
        linked = linked + jnp.where(lower == height, nearby[height], 0)
    spacing = jnp.abs(local_bin[:, None] - local_bin[None, :])
    paired = valid[:, None] & valid[None, :]
    allowed = paired & ((spacing == 0) | (spacing == 1) & (linked == 1))
    allowed = allowed | (position[:, None] == position[None, :])
    return allowed.astype(jnp.float32)


def contrast(query_rows, key_matrix, allowed, valid):
    similarity_scores = (
        lax.dot_general(
            query_rows, key_matrix, (((1,), (1,)), ((), ())), preferred_element_type=jnp.float32
        )
        / SOFTMAX_TEMP_SCALE
    )
    weights = allowed * jnp.exp(similarity_scores)
    shares = weights / jnp.sum(weights, axis=1, keepdims=True)
    position = jnp.arange(query_rows.shape[0], dtype=jnp.int32)
    diagonal = (position[:, None] == position[None, :]).astype(jnp.float32)
    logit_gradient = ((shares - diagonal) * valid[:, None]).astype(jnp.bfloat16)
    query_gradient = (
        jnp.dot(logit_gradient, key_matrix, preferred_element_type=jnp.float32) / SOFTMAX_TEMP_SCALE
    ).astype(jnp.bfloat16)
    key_gradient_rows = (
        lax.dot_general(
            logit_gradient, query_rows, (((0,), (0,)), ((), ())), preferred_element_type=jnp.float32
        )
        / SOFTMAX_TEMP_SCALE
    ).astype(jnp.bfloat16)
    return jnp.stack([query_gradient, key_gradient_rows], axis=1)


def local(features, head_weight, bin_of_row, bin_owner, bin_link):
    rows_dev, views, feat_dim = features.shape
    part_rows, emb_dim = head_weight.shape
    sources = lax.axis_size("dp")
    bin_count = bin_owner.shape[0]
    per_bin = max(2, 2 * rows_dev // bin_count)
    per_owner = per_bin * MOSTB
    group_slots = sources * per_owner
    flat = features.reshape(rows_dev * views, feat_dim)
    columns = flat
    folded = jnp.dot(
        columns,
        lax.all_gather(head_weight, "bin", axis=0, tiled=True),
        preferred_element_type=jnp.float32,
    )
    embedded = folded.reshape(rows_dev, views, emb_dim)
    scale = lax.rsqrt(jnp.sum(embedded * embedded, axis=2, keepdims=True) + 1e-06)
    unit = embedded * scale
    sent = unit.astype(jnp.bfloat16)
    row_bins = bin_of_row[:, 0]
    lookup = row_bins[:, None] == jnp.arange(bin_count, dtype=jnp.int32)[None, :]
    owner = jnp.sum(jnp.where(lookup, bin_owner[None, :], 0), axis=1)
    first_by_bin = jnp.sum((bin_owner[None, :] < bin_owner[:, None]).astype(jnp.int32), axis=1)
    local_bin = row_bins - jnp.sum(jnp.where(lookup, first_by_bin[None, :], 0), axis=1)
    order = jnp.arange(rows_dev, dtype=jnp.int32)
    earlier = (row_bins[:, None] == row_bins[None, :]) & (order[None, :] < order[:, None])
    seat = jnp.sum(earlier.astype(jnp.int32), axis=1)
    target = owner * per_owner + local_bin * per_bin + seat
    outbox = jnp.zeros((group_slots, views, emb_dim), jnp.bfloat16).at[target].set(sent)
    filled = (
        jnp.zeros((group_slots,), jnp.bfloat16).at[target].set(jnp.ones((rows_dev,), jnp.bfloat16))
    )
    inbox, present = (
        lax.all_to_all(
            outbox.reshape(sources, per_owner, views, emb_dim),
            "dp",
            split_axis=0,
            concat_axis=0,
            tiled=True,
        ),
        lax.all_to_all(
            filled.reshape(sources, per_owner), "dp", split_axis=0, concat_axis=0, tiled=True
        ),
    )
    inbox = inbox.reshape(group_slots, views, emb_dim)
    valid = present.reshape(group_slots) > 0.5
    first = jnp.sum((bin_owner < lax.axis_index("dp")).astype(jnp.int32))
    allowed = allowed_mask(valid, first, bin_link, group_slots, per_bin)
    grads = contrast(inbox[:, 0], inbox[:, 1], allowed, valid.astype(jnp.float32))
    returned = lax.all_to_all(
        grads.reshape(sources, per_owner, views, emb_dim),
        "dp",
        split_axis=0,
        concat_axis=0,
        tiled=True,
    )
    row_grads = returned.reshape(group_slots, views, emb_dim)[target].astype(jnp.float32)
    grad_rows = (
        scale * (row_grads - unit * jnp.sum(unit * row_grads, axis=2, keepdims=True))
    ).astype(jnp.bfloat16)
    column_start = lax.axis_index("bin") * part_rows
    trunk = lax.all_gather(features, "bin", axis=0, tiled=True)
    outgrad = lax.all_gather(grad_rows, "bin", axis=0, tiled=True)
    columns = lax.dynamic_slice_in_dim(trunk, column_start, part_rows, 2)
    count = trunk.shape[0]
    local_grad = lax.dot_general(
        columns.reshape(count * views, part_rows),
        outgrad.reshape(count * views, emb_dim),
        (((0,), (0,)), ((), ())),
        preferred_element_type=jnp.float32,
    )
    grad_weight = lax.psum_scatter(local_grad, "dp", scatter_dimension=0, tiled=True) / rows_dev
    return (grad_rows, grad_weight)


WIDTHS = (128, 256, 256, 256, 128)
CHUNKS = len(WIDTHS)
MESH = pl.DeviceIdType.MESH
F32 = jnp.float32
BF16 = jnp.bfloat16


def owners_kernel(
    n_dp, block, per_bin, rows_dev,
    feat, weight, row_bin, bin_owner, bin_link,
    out_rows, out_weight,
    wbuf, fcols, outbox, inbox, flag_out, flag_in, grads, returned, gathered,
    terms, terms16, from_x, pairs, pairs16, from_z,
    w_send, w_recv, f_send, f_recv, flag_send, flag_recv, a_send, a_recv,
    b_send, b_recv, g_send, g_recv, x_send, x_recv, z_send, z_recv,
):
    dp = lax.axis_index("dp")
    col = lax.axis_index("bin")
    half, core = col // 2, col % 2
    sib = half * 2 + (1 - core)
    peer = (1 - half) * 2 + core
    diag = (1 - half) * 2 + (1 - core)
    near = (col, sib, peer, diag)
    ahead = [lax.rem(dp + m, n_dp) for m in range(n_dp)]
    behind = [lax.rem(dp + n_dp - m, n_dp) for m in range(n_dp)]
    rows2, feat_dim = feat.shape
    part = weight.shape[0]
    emb = weight.shape[1]
    slots = n_dp * block
    piece = part // n_dp
    bins = bin_owner.shape[0]
    sends = []

    def push(src, dst, send, recv, device):
        copy = pltpu.make_async_remote_copy(
            src_ref=src, dst_ref=dst, send_sem=send, recv_sem=recv,
            device_id=device, device_id_type=MESH,
        )
        copy.start()
        sends.append(copy)
        return copy

    barrier = pltpu.get_barrier_semaphore()
    for other in near[1:]:
        pl.semaphore_signal(barrier, inc=1, device_id=(dp, other), device_id_type=MESH)
    for m in range(1, n_dp):
        pl.semaphore_signal(barrier, inc=1, device_id=(ahead[m], col), device_id_type=MESH)
    pl.semaphore_wait(barrier, 3 + n_dp - 1)

    lanes = [pl.ds(sum(WIDTHS[:k]), WIDTHS[k]) for k in range(CHUNKS)]
    own_w = []
    for k in range(CHUNKS):
        to_peer = push(
            weight.at[:, lanes[k]], wbuf.at[1, :, lanes[k]],
            w_send.at[1, k], w_recv.at[1, k], (dp, peer),
        )
        to_sib = push(
            weight.at[:, lanes[k]], wbuf.at[0, :, lanes[k]],
            w_send.at[0, k], w_recv.at[0, k], (dp, sib),
        )
        own_w.append((to_sib, to_peer))

    pos = lax.broadcasted_iota(jnp.int32, (rows_dev, rows2), 0)
    lane_row = lax.broadcasted_iota(jnp.int32, (rows_dev, rows2), 1) // 2
    bin_col = jnp.broadcast_to(row_bin[...], (rows_dev, rows2))
    bin_row = jnp.sum(jnp.where(pos == lane_row, bin_col, 0), axis=0, keepdims=True)
    seat = jnp.sum(
        jnp.where((bin_col == bin_row) & (pos < lane_row), 1, 0), axis=0, keepdims=True
    )
    target = seat
    link = jnp.int32(0)
    for b in range(bins):
        owner = bin_owner[b]
        local_bin = jnp.int32(0)
        for b2 in range(b):
            local_bin = local_bin + jnp.where(bin_owner[b2] == owner, 1, 0)
        away = owner - dp
        away = jnp.where(away < 0, away + n_dp, away)
        target = target + jnp.where(bin_row == b, away * block + local_bin * per_bin, 0)
        if b + 1 < bins:
            link = link + jnp.where((owner == dp) & (local_bin == 0), bin_link[b], 0)
    place = lax.broadcasted_iota(jnp.int32, (slots, rows2), 0)
    view = lax.broadcasted_iota(jnp.int32, (slots, rows2), 1) % 2
    here = place == jnp.broadcast_to(target, (slots, rows2))
    pick = [
        jnp.where(here & (view == v), 1.0, 0.0).astype(F32) for v in range(2)
    ]
    flags = jnp.broadcast_to(jnp.sum(pick[0], axis=1, keepdims=True), (slots, 128)).astype(BF16)
    pick = [p.astype(BF16) for p in pick]
    flag_out[...] = flags
    flag_in[0:block, :] = flags[0:block]
    flag_copies = []
    for m in range(1, n_dp):
        span = pl.ds(m * block, block)
        flag_copies.append(push(
            flag_out.at[span], flag_in.at[span], flag_send.at[m], flag_recv.at[m],
            (ahead[m], col),
        ))

    order = list(range(n_dp - 1, 0, -1))

    def start_out(k):
        copies = []
        for m in order:
            span = pl.ds(m * block, block)
            copies.append(push(
                outbox.at[:, span, lanes[k]], inbox.at[:, span, lanes[k]],
                a_send.at[k, m], a_recv.at[k, m], (ahead[m], col),
            ))
        return copies

    def columns_of(other):
        return pl.ds(pl.multiple_of(other * part, part), part)

    out_copies = []
    for k in range(CHUNKS):
        to_sib, to_peer = own_w[k]
        to_peer.wait_recv()
        relay = push(
            wbuf.at[1, :, lanes[k]], wbuf.at[2, :, lanes[k]],
            w_send.at[2, k], w_recv.at[2, k], (dp, sib),
        )
        y = jnp.dot(feat[:, columns_of(col)], weight[:, lanes[k]], preferred_element_type=F32)
        y += jnp.dot(feat[:, columns_of(peer)], wbuf[1, :, lanes[k]], preferred_element_type=F32)
        to_sib.wait_recv()
        y += jnp.dot(feat[:, columns_of(sib)], wbuf[0, :, lanes[k]], preferred_element_type=F32)
        relay.wait_recv()
        y += jnp.dot(feat[:, columns_of(diag)], wbuf[2, :, lanes[k]], preferred_element_type=F32)
        y = y.astype(BF16)
        for v in range(2):
            placed = jnp.dot(pick[v], y, preferred_element_type=F32).astype(BF16)
            outbox[v, :, lanes[k]] = placed
            inbox[v, 0:block, lanes[k]] = placed[0:block]
        out_copies.append(start_out(k))

    f_copies = []
    for x in (2, 3, 1):
        f_copies.append(push(
            feat.at[:, columns_of(near[x])], fcols.at[pl.ds(x * rows2, rows2), :],
            f_send.at[x], f_recv.at[x], (dp, near[x]),
        ))
    fcols[0:rows2, :] = feat[:, columns_of(col)]

    for copy in flag_copies:
        copy.wait_recv()
    raw = jnp.zeros((slots, slots), F32)
    square = [jnp.zeros((slots, 1), F32) for _ in range(2)]
    for k in range(CHUNKS):
        for copy in out_copies[k]:
            copy.wait_recv()
        raw += lax.dot_general(
            inbox[0, :, lanes[k]], inbox[1, :, lanes[k]], (((1,), (1,)), ((), ())), preferred_element_type=F32
        )
        for v in range(2):
            row = inbox[v, :, lanes[k]].astype(F32)
            square[v] += jnp.sum(row * row, axis=1, keepdims=True)
    scale0 = lax.rsqrt(square[0] + 1e-06)
    scale1 = lax.rsqrt(square[1] + 1e-06)
    s_pos = lax.broadcasted_iota(jnp.int32, (slots, slots), 0)
    t_pos = lax.broadcasted_iota(jnp.int32, (slots, slots), 1)
    eye = s_pos == t_pos
    scale1_row = jnp.sum(jnp.where(eye, scale1, 0.0), axis=0, keepdims=True)
    valid = flag_in[:, 0:1].astype(F32)
    valid_row = jnp.sum(jnp.where(eye, valid, 0.0), axis=0, keepdims=True)
    s_bin = (lax.broadcasted_iota(jnp.int32, (slots, 1), 0) % block >= per_bin).astype(jnp.int32)
    t_bin = (lax.broadcasted_iota(jnp.int32, (1, slots), 1) % block >= per_bin).astype(jnp.int32)
    bound = jnp.where(s_bin == t_bin, 1.0, (link == 1).astype(F32))
    allowed = jnp.where(eye, 1.0, valid * valid_row * bound)
    scores = raw * scale0 * scale1_row / SOFTMAX_TEMP_SCALE
    weights = allowed * jnp.exp(scores)
    shares = weights / jnp.sum(weights, axis=1, keepdims=True)
    logit = ((shares - jnp.where(eye, 1.0, 0.0)) * valid).astype(BF16).astype(F32)
    slope = logit * scores
    lean0 = jnp.sum(slope, axis=1, keepdims=True) * scale0 * scale0
    lean1_row = jnp.sum(slope, axis=0, keepdims=True) * scale1_row * scale1_row
    lean1 = jnp.sum(jnp.where(eye, lean1_row, 0.0), axis=1, keepdims=True)
    mix = logit * scale0 * scale1_row / SOFTMAX_TEMP_SCALE
    high = mix.astype(BF16)
    low = (mix - high.astype(F32)).astype(BF16)
    high_t, low_t = high.T, low.T

    back_copies = []
    for k in range(CHUNKS):
        y0, y1 = inbox[0, :, lanes[k]], inbox[1, :, lanes[k]]
        g0 = jnp.dot(high, y1, preferred_element_type=F32)
        g0 += jnp.dot(low, y1, preferred_element_type=F32) - lean0 * y0.astype(F32)
        g1 = jnp.dot(high_t, y0, preferred_element_type=F32)
        g1 += jnp.dot(low_t, y0, preferred_element_type=F32) - lean1 * y1.astype(F32)
        for v, g in ((0, g0.astype(BF16)), (1, g1.astype(BF16))):
            grads[v, :, lanes[k]] = g
            returned[v, 0:block, lanes[k]] = g[0:block]
        copies = []
        for m in order:
            span = pl.ds(m * block, block)
            copies.append(push(
                grads.at[:, span, lanes[k]], returned.at[:, span, lanes[k]],
                b_send.at[k, m], b_recv.at[k, m], (behind[m], col),
            ))
        back_copies.append(copies)

    for copy in f_copies:
        copy.wait_recv()
    across = (dp // 2) * 2 + (1 - dp % 2)
    layer, side = dp // 2, dp % 2
    layers = n_dp // 2
    x_copies, z_copies = [], []

    def finish_pair(k):
        x_copies[k].wait_recv()
        pair = terms[:, side, :, lanes[k]] + from_x[:, :, lanes[k]].astype(F32)
        pairs[:, :, lanes[k]] = pair
        pairs16[:, :, lanes[k]] = pair.astype(BF16)
        copies = []
        for step in range(layers - 1, 0, -1):
            to = lax.rem(layer + step, layers)
            copies.append(push(
                pairs16.at[to, :, lanes[k]], from_z.at[step, :, lanes[k]],
                z_send.at[k, step], z_recv.at[k, step], (to * 2 + side, col),
            ))
        z_copies.append(copies)

    for k in range(CHUNKS):
        for copy in back_copies[k]:
            copy.wait_recv()
        rows = jnp.zeros((rows2, WIDTHS[k]), F32)
        for v in range(2):
            rows += lax.dot_general(
                pick[v], returned[v, :, lanes[k]], (((0,), (0,)), ((), ())), preferred_element_type=F32
            )
        rows = rows.astype(BF16)
        out_rows[:, lanes[k]] = rows
        gathered[0:rows2, lanes[k]] = rows
        own = gathered.at[pl.ds(0, rows2), lanes[k]]
        spans = [pl.ds(x * rows2, rows2) for x in range(4)]
        to_peer = push(
            own, gathered.at[spans[2], lanes[k]], g_send.at[1, k], g_recv.at[1, k], (dp, peer)
        )
        to_sib = push(
            own, gathered.at[spans[1], lanes[k]], g_send.at[0, k], g_recv.at[0, k], (dp, sib)
        )
        if k > 0:
            finish_pair(k - 1)
        to_peer.wait_recv()
        relay = push(
            gathered.at[spans[2], lanes[k]], gathered.at[spans[3], lanes[k]],
            g_send.at[2, k], g_recv.at[2, k], (dp, sib),
        )
        to_sib.wait_recv()
        relay.wait_recv()
        term = lax.dot_general(
            fcols[...], gathered[:, lanes[k]], (((0,), (0,)), ((), ())), preferred_element_type=F32
        )
        term = term.reshape(layers, 2, piece, WIDTHS[k])
        terms[:, :, :, lanes[k]] = term
        terms16[:, :, :, lanes[k]] = term.astype(BF16)
        x_copies.append(push(
            terms16.at[:, 1 - side, :, lanes[k]], from_x.at[:, :, lanes[k]],
            x_send.at[k], x_recv.at[k], (across, col),
        ))
    finish_pair(CHUNKS - 1)
    for k in range(CHUNKS):
        total = pairs[layer, :, lanes[k]]
        for copy in z_copies[k]:
            copy.wait_recv()
        for step in range(1, layers):
            total += from_z[step, :, lanes[k]].astype(F32)
        out_weight[:, lanes[k]] = total / rows_dev
    for copy in sends:
        copy.wait_send()


def local_kernel(features, head_weight, bin_of_row, bin_owner, bin_link):
    rows_dev, views, feat_dim = features.shape
    part, emb = head_weight.shape
    n_dp = lax.axis_size("dp")
    bins = bin_owner.shape[0]
    per_bin = max(2, 2 * rows_dev // bins)
    block = -(-per_bin * MOSTB // 16) * 16
    slots = n_dp * block
    rows2 = rows_dev * views
    layers = n_dp // 2
    piece = part // n_dp
    vmem = pl.BlockSpec(memory_space=pltpu.VMEM)
    smem = pl.BlockSpec(memory_space=pltpu.SMEM)
    dma = pltpu.SemaphoreType.DMA
    wide = pltpu.VMEM((views, slots, emb), BF16)
    grad_rows, grad_weight = pl.pallas_call(
        functools.partial(owners_kernel, n_dp, block, per_bin, rows_dev),
        out_shape=(
            jax.ShapeDtypeStruct((rows2, emb), BF16),
            jax.ShapeDtypeStruct((piece, emb), F32),
        ),
        in_specs=[vmem, vmem, vmem, smem, smem],
        out_specs=(vmem, vmem),
        scratch_shapes=[
            pltpu.VMEM((3, part, emb), BF16),
            pltpu.VMEM((4 * rows2, part), BF16),
            wide, wide,
            pltpu.VMEM((slots, 128), BF16),
            pltpu.VMEM((slots, 128), BF16),
            wide, wide,
            pltpu.VMEM((4 * rows2, emb), BF16),
            pltpu.VMEM((layers, 2, piece, emb), F32),
            pltpu.VMEM((layers, 2, piece, emb), BF16),
            pltpu.VMEM((layers, piece, emb), BF16),
            pltpu.VMEM((layers, piece, emb), F32),
            pltpu.VMEM((layers, piece, emb), BF16),
            pltpu.VMEM((layers, piece, emb), BF16),
            dma((3, CHUNKS)), dma((3, CHUNKS)),
            dma((4,)), dma((4,)),
            dma((n_dp,)), dma((n_dp,)),
            dma((CHUNKS, n_dp)), dma((CHUNKS, n_dp)),
            dma((CHUNKS, n_dp)), dma((CHUNKS, n_dp)),
            dma((3, CHUNKS)), dma((3, CHUNKS)),
            dma((CHUNKS,)), dma((CHUNKS,)),
            dma((CHUNKS, layers)), dma((CHUNKS, layers)),
        ],
        compiler_params=pltpu.CompilerParams(
            collective_id=0, has_side_effects=True, vmem_limit_bytes=48 * 1024 * 1024
        ),
        cost_estimate=pl.CostEstimate(
            flops=4 * rows2 * feat_dim * emb, bytes_accessed=16 * 1024 * 1024, transcendentals=0
        ),
    )(features.reshape(rows2, feat_dim), head_weight, bin_of_row, bin_owner, bin_link)
    return grad_rows.reshape(rows_dev, views, emb), grad_weight


def solution(mesh):
    small = mesh.shape["dp"] <= 8 and mesh.shape["bin"] == 4
    return jax.shard_map(
        local_kernel if small else local,
        mesh=mesh,
        in_specs=(P(("dp", "bin"), None, None), P("bin", None), P(("dp", "bin"), None), P(), P()),
        out_specs=(P(("dp", "bin"), None, None), P(("bin", "dp"), None)),
        check_vma=False,
    )
```

profile of v0, /device:TPU:0, one launch (start us, length us, event | category | flops | bytes accessed | tf_op | source)
XLA Modules:
  0.0 116.5 jit_solution(5499667174903473671)
XLA Ops:
  0.6 0.8 copy.7.row_bin
  1.4 0.0 copy-start
  1.4 0.0 copy-start.1
  1.4 0.0 copy-start.2
  1.4 1.6 %reshape.10.feat = bf16[256,2048]{1,0:T(8,128)(2,1)S(1)} reshape(bf16[128,2,2048]{2,1,0:T(2,128)(2,1)} %param.5) | data formatting | bytes 2097152 | tf_op jit(solution)/shard_map/reshape | solution.py:455
  3.0 0.0 copy-done
  3.0 0.0 copy-done.1
  3.0 0.0 copy-done.2
  3.0 111.8 %shard_map.68 = (bf16[256,1024]{1,0:T(8,128)(2,1)S(1)}, f32[64,1024]{1,0:T(8,128)S(1)}) custom-call(bf16[256,2048]{1,0:T(8,128)(2,1)S(1)} %reshape.10.feat, bf16[512,1024]{1,0:T(8,128)(2,1)S(1)} %copy-done, s32[128,1]{1,0:T(8,128)S(1)} %copy.7.row_bin, s32[12]{0:T(128)S(1)} %copy-done.1, s32[12]{0:T(128)S(1)} %copy-done.2), custom_call_target="tpu_custom_call" | custom-call | flops 2147483648 | bytes 16777216 | tf_op jit(solution)/shard_map/pallas_call | solution.py:418
  114.9 1.0 reshape.11
  115.8 0.7 copy.9
Async XLA Ops:
  1.4 1.6 %copy-start = (bf16[512,1024]{1,0:T(8,128)(2,1)S(1)}, bf16[512,1024]{1,0:T(8,128)(2,1)}, u32[]{:S(2)}) copy-start(bf16[512,1024]{1,0:T(8,128)(2,1)} %weight.1) | copy-start | bytes 3145732
  1.4 1.6 %copy-start.1 = (s32[12]{0:T(128)S(1)}, s32[12]{0:T(128)}, u32[]{:S(2)}) copy-start(s32[12]{0:T(128)} %bin_owner.1) | copy-start | bytes 148
  1.4 1.6 %copy-start.2 = (s32[12]{0:T(128)S(1)}, s32[12]{0:T(128)}, u32[]{:S(2)}) copy-start(s32[12]{0:T(128)} %bin_link.1) | copy-start | bytes 148
where the time goes:
time: 117 us
  Pallas kernels  112 us (96%)
  local copies, waits for them, and re-layouts  4.02 us (3%)
    pallas_call x1, Pallas kernels, local_kernel(): pl.pallas_call(functools.partial(owners_kernel, n_dp, block, per_bin, row...  112 us

commit v1 on v0

--- a/solution.py
+++ b/solution.py
@@ -131,6 +131,7 @@
 
 WIDTHS = (128, 256, 256, 256, 128)
 CHUNKS = len(WIDTHS)
+AHEAD = 2
 MESH = pl.DeviceIdType.MESH
 F32 = jnp.float32
 BF16 = jnp.bfloat16
@@ -180,7 +181,8 @@
 
     lanes = [pl.ds(sum(WIDTHS[:k]), WIDTHS[k]) for k in range(CHUNKS)]
     own_w = []
-    for k in range(CHUNKS):
+
+    def start_weight(k):
         to_peer = push(
             weight.at[:, lanes[k]], wbuf.at[1, :, lanes[k]],
             w_send.at[1, k], w_recv.at[1, k], (dp, peer),
@@ -190,6 +192,9 @@
             w_send.at[0, k], w_recv.at[0, k], (dp, sib),
         )
         own_w.append((to_sib, to_peer))
+
+    for k in range(AHEAD):
+        start_weight(k)
 
     pos = lax.broadcasted_iota(jnp.int32, (rows_dev, rows2), 0)
     lane_row = lax.broadcasted_iota(jnp.int32, (rows_dev, rows2), 1) // 2
@@ -247,6 +252,8 @@
     for k in range(CHUNKS):
         to_sib, to_peer = own_w[k]
         to_peer.wait_recv()
+        if k + AHEAD < CHUNKS:
+            start_weight(k + AHEAD)
         relay = push(
             wbuf.at[1, :, lanes[k]], wbuf.at[2, :, lanes[k]],
             w_send.at[2, k], w_recv.at[2, k], (dp, sib),
@@ -311,7 +318,8 @@
     high_t, low_t = high.T, low.T
 
     back_copies = []
-    for k in range(CHUNKS):
+
+    def start_back(k):
         y0, y1 = inbox[0, :, lanes[k]], inbox[1, :, lanes[k]]
         g0 = jnp.dot(high, y1, preferred_element_type=F32)
         g0 += jnp.dot(low, y1, preferred_element_type=F32) - lean0 * y0.astype(F32)
@@ -329,6 +337,9 @@
             ))
         back_copies.append(copies)
 
+    for k in range(AHEAD):
+        start_back(k)
+
     for copy in f_copies:
         copy.wait_recv()
     across = (dp // 2) * 2 + (1 - dp % 2)
@@ -353,6 +364,8 @@
     for k in range(CHUNKS):
         for copy in back_copies[k]:
             copy.wait_recv()
+        if k + AHEAD < CHUNKS:
+            start_back(k + AHEAD)
         rows = jnp.zeros((rows2, WIDTHS[k]), F32)
         for v in range(2):
             rows += lax.dot_general(

time: 117 us -> 117 us (level)
  no operation moved by 1% of the time
where the time goes in v1:
time: 117 us
  Pallas kernels  113 us (97%)
  local copies, waits for them, and re-layouts  4.02 us (3%)
    pallas_call x1, Pallas kernels, local_kernel(): pl.pallas_call(functools.partial(owners_kernel, n_dp, block, per_bin, row...  113 us

profile of v1, /device:TPU:0, one launch (start us, length us, event | category | flops | bytes accessed | tf_op | source)
XLA Modules:
  0.0 117.2 jit_solution(2985769413093610873)
XLA Ops:
  0.6 0.8 copy.7.row_bin
  1.4 0.0 copy-start
  1.4 0.0 copy-start.1
  1.4 0.0 copy-start.2
  1.4 1.6 %reshape.10.feat = bf16[256,2048]{1,0:T(8,128)(2,1)S(1)} reshape(bf16[128,2,2048]{2,1,0:T(2,128)(2,1)} %param.5) | data formatting | bytes 2097152 | tf_op jit(solution)/shard_map/reshape | solution.py:468
  3.0 0.0 copy-done
  3.0 0.0 copy-done.1
  3.0 0.0 copy-done.2
  3.0 112.5 %shard_map.68 = (bf16[256,1024]{1,0:T(8,128)(2,1)S(1)}, f32[64,1024]{1,0:T(8,128)S(1)}) custom-call(bf16[256,2048]{1,0:T(8,128)(2,1)S(1)} %reshape.10.feat, bf16[512,1024]{1,0:T(8,128)(2,1)S(1)} %copy-done, s32[128,1]{1,0:T(8,128)S(1)} %copy.7.row_bin, s32[12]{0:T(128)S(1)} %copy-done.1, s32[12]{0:T(128)S(1)} %copy-done.2), custom_call_target="tpu_custom_call" | custom-call | flops 2147483648 | bytes 16777216 | tf_op jit(solution)/shard_map/pallas_call | solution.py:431
  115.5 1.0 reshape.11
  116.5 0.7 copy.9
Async XLA Ops:
  1.4 1.6 %copy-start = (bf16[512,1024]{1,0:T(8,128)(2,1)S(1)}, bf16[512,1024]{1,0:T(8,128)(2,1)}, u32[]{:S(2)}) copy-start(bf16[512,1024]{1,0:T(8,128)(2,1)} %weight.1) | copy-start | bytes 3145732
  1.4 1.6 %copy-start.1 = (s32[12]{0:T(128)S(1)}, s32[12]{0:T(128)}, u32[]{:S(2)}) copy-start(s32[12]{0:T(128)} %bin_owner.1) | copy-start | bytes 148
  1.4 1.6 %copy-start.2 = (s32[12]{0:T(128)S(1)}, s32[12]{0:T(128)}, u32[]{:S(2)}) copy-start(s32[12]{0:T(128)} %bin_link.1) | copy-start | bytes 148

commit v2 on v0

--- a/solution.py
+++ b/solution.py
@@ -140,7 +140,7 @@
     n_dp, block, per_bin, rows_dev,
     feat, weight, row_bin, bin_owner, bin_link,
     out_rows, out_weight,
-    wbuf, fcols, outbox, inbox, flag_out, flag_in, grads, returned, gathered,
+    wbuf, fcols, fcols_t, outbox, inbox, flag_out, flag_in, grads, returned, gathered,
     terms, terms16, from_x, pairs, pairs16, from_z,
     w_send, w_recv, f_send, f_recv, flag_send, flag_recv, a_send, a_recv,
     b_send, b_recv, g_send, g_recv, x_send, x_recv, z_send, z_recv,
@@ -217,6 +217,7 @@
         jnp.where(here & (view == v), 1.0, 0.0).astype(F32) for v in range(2)
     ]
     flags = jnp.broadcast_to(jnp.sum(pick[0], axis=1, keepdims=True), (slots, 128)).astype(BF16)
+    pick_t = [p.T.astype(BF16) for p in pick]
     pick = [p.astype(BF16) for p in pick]
     flag_out[...] = flags
     flag_in[0:block, :] = flags[0:block]
@@ -274,30 +275,37 @@
 
     for copy in flag_copies:
         copy.wait_recv()
-    raw = jnp.zeros((slots, slots), F32)
-    square = [jnp.zeros((slots, 1), F32) for _ in range(2)]
-    for k in range(CHUNKS):
-        for copy in out_copies[k]:
-            copy.wait_recv()
-        raw += lax.dot_general(
-            inbox[0, :, lanes[k]], inbox[1, :, lanes[k]], (((1,), (1,)), ((), ())), preferred_element_type=F32
-        )
-        for v in range(2):
-            row = inbox[v, :, lanes[k]].astype(F32)
-            square[v] += jnp.sum(row * row, axis=1, keepdims=True)
-    scale0 = lax.rsqrt(square[0] + 1e-06)
-    scale1 = lax.rsqrt(square[1] + 1e-06)
     s_pos = lax.broadcasted_iota(jnp.int32, (slots, slots), 0)
     t_pos = lax.broadcasted_iota(jnp.int32, (slots, slots), 1)
     eye = s_pos == t_pos
-    scale1_row = jnp.sum(jnp.where(eye, scale1, 0.0), axis=0, keepdims=True)
     valid = flag_in[:, 0:1].astype(F32)
     valid_row = jnp.sum(jnp.where(eye, valid, 0.0), axis=0, keepdims=True)
     s_bin = (lax.broadcasted_iota(jnp.int32, (slots, 1), 0) % block >= per_bin).astype(jnp.int32)
     t_bin = (lax.broadcasted_iota(jnp.int32, (1, slots), 1) % block >= per_bin).astype(jnp.int32)
     bound = jnp.where(s_bin == t_bin, 1.0, (link == 1).astype(F32))
     allowed = jnp.where(eye, 1.0, valid * valid_row * bound)
-    scores = raw * scale0 * scale1_row / SOFTMAX_TEMP_SCALE
+
+    def turn_columns(x):
+        span = pl.ds(x * rows2, rows2)
+        fcols_t[:, span] = fcols[span, :].T
+
+    turn_columns(0)
+    raw = jnp.zeros((slots, slots), F32)
+    square = [jnp.zeros((slots, 1), F32) for _ in range(2)]
+    for k in range(CHUNKS):
+        for copy in out_copies[k]:
+            copy.wait_recv()
+        raw += lax.dot_general(
+            inbox[0, :, lanes[k]], inbox[1, :, lanes[k]], (((1,), (1,)), ((), ())), preferred_element_type=F32
+        )
+        for v in range(2):
+            row = inbox[v, :, lanes[k]].astype(F32)
+            square[v] += jnp.sum(row * row, axis=1, keepdims=True)
+    scale0 = lax.rsqrt(square[0] + 1e-06)
+    scale1 = lax.rsqrt(square[1] + 1e-06)
+    scale1_row = jnp.sum(jnp.where(eye, scale1, 0.0), axis=0, keepdims=True)
+    warm_row = scale1_row * (1.0 / SOFTMAX_TEMP_SCALE)
+    scores = raw * scale0 * warm_row
     weights = allowed * jnp.exp(scores)
     shares = weights / jnp.sum(weights, axis=1, keepdims=True)
     logit = ((shares - jnp.where(eye, 1.0, 0.0)) * valid).astype(BF16).astype(F32)
@@ -305,7 +313,7 @@
     lean0 = jnp.sum(slope, axis=1, keepdims=True) * scale0 * scale0
     lean1_row = jnp.sum(slope, axis=0, keepdims=True) * scale1_row * scale1_row
     lean1 = jnp.sum(jnp.where(eye, lean1_row, 0.0), axis=1, keepdims=True)
-    mix = logit * scale0 * scale1_row / SOFTMAX_TEMP_SCALE
+    mix = logit * scale0 * warm_row
     high = mix.astype(BF16)
     low = (mix - high.astype(F32)).astype(BF16)
     high_t, low_t = high.T, low.T
@@ -329,8 +337,9 @@
             ))
         back_copies.append(copies)
 
-    for copy in f_copies:
+    for x, copy in zip((2, 3, 1), f_copies):
         copy.wait_recv()
+        turn_columns(x)
     across = (dp // 2) * 2 + (1 - dp % 2)
     layer, side = dp // 2, dp % 2
     layers = n_dp // 2
@@ -355,9 +364,7 @@
             copy.wait_recv()
         rows = jnp.zeros((rows2, WIDTHS[k]), F32)
         for v in range(2):
-            rows += lax.dot_general(
-                pick[v], returned[v, :, lanes[k]], (((0,), (0,)), ((), ())), preferred_element_type=F32
-            )
+            rows += jnp.dot(pick_t[v], returned[v, :, lanes[k]], preferred_element_type=F32)
         rows = rows.astype(BF16)
         out_rows[:, lanes[k]] = rows
         gathered[0:rows2, lanes[k]] = rows
@@ -378,9 +385,7 @@
         )
         to_sib.wait_recv()
         relay.wait_recv()
-        term = lax.dot_general(
-            fcols[...], gathered[:, lanes[k]], (((0,), (0,)), ((), ())), preferred_element_type=F32
-        )
+        term = jnp.dot(fcols_t[...], gathered[:, lanes[k]], preferred_element_type=F32)
         term = term.reshape(layers, 2, piece, WIDTHS[k])
         terms[:, :, :, lanes[k]] = term
         terms16[:, :, :, lanes[k]] = term.astype(BF16)
@@ -426,6 +431,7 @@
         scratch_shapes=[
             pltpu.VMEM((3, part, emb), BF16),
             pltpu.VMEM((4 * rows2, part), BF16),
+            pltpu.VMEM((part, 4 * rows2), BF16),
             wide, wide,
             pltpu.VMEM((slots, 128), BF16),
             pltpu.VMEM((slots, 128), BF16),

time: 117 us -> 116 us (level)
  no operation moved by 1% of the time
where the time goes in v2:
time: 116 us
  Pallas kernels  112 us (97%)
  local copies, waits for them, and re-layouts  4.02 us (3%)
    pallas_call x1, Pallas kernels, local_kernel(): pl.pallas_call(functools.partial(owners_kernel, n_dp, block, per_bin, row...  112 us

profile of v2, /device:TPU:0, one launch (start us, length us, event | category | flops | bytes accessed | tf_op | source)
XLA Modules:
  0.0 116.2 jit_solution(1064787450920292689)
XLA Ops:
  0.6 0.8 copy.7.row_bin
  1.4 0.0 copy-start
  1.4 0.0 copy-start.1
  1.4 0.0 copy-start.2
  1.4 1.6 %reshape.10.feat = bf16[256,2048]{1,0:T(8,128)(2,1)S(1)} reshape(bf16[128,2,2048]{2,1,0:T(2,128)(2,1)} %param.5) | data formatting | bytes 2097152 | tf_op jit(solution)/shard_map/reshape | solution.py:461
  3.0 0.0 copy-done
  3.0 0.0 copy-done.1
  3.0 0.0 copy-done.2
  3.0 111.5 %shard_map.68 = (bf16[256,1024]{1,0:T(8,128)(2,1)S(1)}, f32[64,1024]{1,0:T(8,128)S(1)}) custom-call(bf16[256,2048]{1,0:T(8,128)(2,1)S(1)} %reshape.10.feat, bf16[512,1024]{1,0:T(8,128)(2,1)S(1)} %copy-done, s32[128,1]{1,0:T(8,128)S(1)} %copy.7.row_bin, s32[12]{0:T(128)S(1)} %copy-done.1, s32[12]{0:T(128)S(1)} %copy-done.2), custom_call_target="tpu_custom_call" | custom-call | flops 2147483648 | bytes 16777216 | tf_op jit(solution)/shard_map/pallas_call | solution.py:423
  114.5 1.0 reshape.11
  115.5 0.7 copy.9
Async XLA Ops:
  1.4 1.6 %copy-start = (bf16[512,1024]{1,0:T(8,128)(2,1)S(1)}, bf16[512,1024]{1,0:T(8,128)(2,1)}, u32[]{:S(2)}) copy-start(bf16[512,1024]{1,0:T(8,128)(2,1)} %weight.1) | copy-start | bytes 3145732
  1.4 1.6 %copy-start.1 = (s32[12]{0:T(128)S(1)}, s32[12]{0:T(128)}, u32[]{:S(2)}) copy-start(s32[12]{0:T(128)} %bin_owner.1) | copy-start | bytes 148
  1.4 1.6 %copy-start.2 = (s32[12]{0:T(128)S(1)}, s32[12]{0:T(128)}, u32[]{:S(2)}) copy-start(s32[12]{0:T(128)} %bin_link.1) | copy-start | bytes 148

commit v3 on v2

--- a/solution.py
+++ b/solution.py
@@ -136,6 +136,14 @@
 BF16 = jnp.bfloat16
 
 
+def mixed(a, b, n):
+    total, unit = 0, 1
+    while unit < n:
+        total = total + (a // unit + b // unit) % 2 * unit
+        unit *= 2
+    return total
+
+
 def owners_kernel(
     n_dp, block, per_bin, rows_dev,
     feat, weight, row_bin, bin_owner, bin_link,
@@ -152,8 +160,11 @@
     peer = (1 - half) * 2 + core
     diag = (1 - half) * 2 + (1 - core)
     near = (col, sib, peer, diag)
-    ahead = [lax.rem(dp + m, n_dp) for m in range(n_dp)]
-    behind = [lax.rem(dp + n_dp - m, n_dp) for m in range(n_dp)]
+    far = list(range(n_dp // 2, n_dp))
+    close = list(range(1, n_dp // 2))
+    first_core = [m for pair in zip(far, close) for m in pair] + far[len(close):]
+    other_core = [m for pair in zip(close, far) for m in pair] + far[len(close):]
+    turns = [a + core * (b - a) for a, b in zip(first_core, other_core)]
     rows2, feat_dim = feat.shape
     part = weight.shape[0]
     emb = weight.shape[1]
@@ -175,7 +186,7 @@
     for other in near[1:]:
         pl.semaphore_signal(barrier, inc=1, device_id=(dp, other), device_id_type=MESH)
     for m in range(1, n_dp):
-        pl.semaphore_signal(barrier, inc=1, device_id=(ahead[m], col), device_id_type=MESH)
+        pl.semaphore_signal(barrier, inc=1, device_id=(mixed(dp, m, n_dp), col), device_id_type=MESH)
     pl.semaphore_wait(barrier, 3 + n_dp - 1)
 
     lanes = [pl.ds(sum(WIDTHS[:k]), WIDTHS[k]) for k in range(CHUNKS)]
@@ -205,8 +216,7 @@
         local_bin = jnp.int32(0)
         for b2 in range(b):
             local_bin = local_bin + jnp.where(bin_owner[b2] == owner, 1, 0)
-        away = owner - dp
-        away = jnp.where(away < 0, away + n_dp, away)
+        away = mixed(owner, dp, n_dp)
         target = target + jnp.where(bin_row == b, away * block + local_bin * per_bin, 0)
         if b + 1 < bins:
             link = link + jnp.where((owner == dp) & (local_bin == 0), bin_link[b], 0)
@@ -226,19 +236,22 @@
         span = pl.ds(m * block, block)
         flag_copies.append(push(
             flag_out.at[span], flag_in.at[span], flag_send.at[m], flag_recv.at[m],
-            (ahead[m], col),
+            (mixed(dp, m, n_dp), col),
         ))
 
-    order = list(range(n_dp - 1, 0, -1))
-
-    def start_out(k):
-        copies = []
-        for m in order:
-            span = pl.ds(m * block, block)
-            copies.append(push(
-                outbox.at[:, span, lanes[k]], inbox.at[:, span, lanes[k]],
-                a_send.at[k, m], a_recv.at[k, m], (ahead[m], col),
-            ))
+    def exchange(src, dst, send, recv, k):
+        def block_copy(m):
+            span = pl.ds(pl.multiple_of(m * block, block), block)
+            return pltpu.make_async_remote_copy(
+                src_ref=src.at[:, span, lanes[k]], dst_ref=dst.at[:, span, lanes[k]],
+                send_sem=send.at[k, m], recv_sem=recv.at[k, m],
+                device_id=(mixed(dp, m, n_dp), col), device_id_type=MESH,
+            )
+
+        for m in turns:
+            block_copy(m).start()
+        copies = [block_copy(m) for m in range(1, n_dp)]
+        sends.extend(copies)
         return copies
 
     def columns_of(other):
@@ -263,7 +276,7 @@
             placed = jnp.dot(pick[v], y, preferred_element_type=F32).astype(BF16)
             outbox[v, :, lanes[k]] = placed
             inbox[v, 0:block, lanes[k]] = placed[0:block]
-        out_copies.append(start_out(k))
+        out_copies.append(exchange(outbox, inbox, a_send, a_recv, k))
 
     f_copies = []
     for x in (2, 3, 1):
@@ -328,14 +341,7 @@
         for v, g in ((0, g0.astype(BF16)), (1, g1.astype(BF16))):
             grads[v, :, lanes[k]] = g
             returned[v, 0:block, lanes[k]] = g[0:block]
-        copies = []
-        for m in order:
-            span = pl.ds(m * block, block)
-            copies.append(push(
-                grads.at[:, span, lanes[k]], returned.at[:, span, lanes[k]],
-                b_send.at[k, m], b_recv.at[k, m], (behind[m], col),
-            ))
-        back_copies.append(copies)
+        back_copies.append(exchange(grads, returned, b_send, b_recv, k))
 
     for x, copy in zip((2, 3, 1), f_copies):
         copy.wait_recv()

time: 116 us -> 116 us (level)
  no operation moved by 1% of the time
where the time goes in v3:
time: 116 us; the launch traced here: 115 us
  Pallas kernels  111 us (96%)
  local copies, waits for them, and re-layouts  4.02 us (3%)
    pallas_call x1, Pallas kernels, local_kernel(): pl.pallas_call(functools.partial(owners_kernel, n_dp, block, per_bin, row...  111 us

profile of v3, /device:TPU:0, one launch (start us, length us, event | category | flops | bytes accessed | tf_op | source)
XLA Modules:
  0.0 115.4 jit_solution(15173847333353116292)
XLA Ops:
  0.6 0.8 copy.7.row_bin
  1.4 0.0 copy-start
  1.4 0.0 copy-start.1
  1.4 0.0 copy-start.2
  1.4 1.6 %reshape.10.feat = bf16[256,2048]{1,0:T(8,128)(2,1)S(1)} reshape(bf16[128,2,2048]{2,1,0:T(2,128)(2,1)} %param.5) | data formatting | bytes 2097152 | tf_op jit(solution)/shard_map/reshape | solution.py:467
  3.0 0.0 copy-done
  3.0 0.0 copy-done.1
  3.0 0.0 copy-done.2
  3.0 110.7 %shard_map.68 = (bf16[256,1024]{1,0:T(8,128)(2,1)S(1)}, f32[64,1024]{1,0:T(8,128)S(1)}) custom-call(bf16[256,2048]{1,0:T(8,128)(2,1)S(1)} %reshape.10.feat, bf16[512,1024]{1,0:T(8,128)(2,1)S(1)} %copy-done, s32[128,1]{1,0:T(8,128)S(1)} %copy.7.row_bin, s32[12]{0:T(128)S(1)} %copy-done.1, s32[12]{0:T(128)S(1)} %copy-done.2), custom_call_target="tpu_custom_call" | custom-call | flops 2147483648 | bytes 16777216 | tf_op jit(solution)/shard_map/pallas_call | solution.py:429
  113.7 1.0 reshape.11
  114.7 0.7 copy.9
Async XLA Ops:
  1.4 1.6 %copy-start = (bf16[512,1024]{1,0:T(8,128)(2,1)S(1)}, bf16[512,1024]{1,0:T(8,128)(2,1)}, u32[]{:S(2)}) copy-start(bf16[512,1024]{1,0:T(8,128)(2,1)} %weight.1) | copy-start | bytes 3145732
  1.4 1.6 %copy-start.1 = (s32[12]{0:T(128)S(1)}, s32[12]{0:T(128)}, u32[]{:S(2)}) copy-start(s32[12]{0:T(128)} %bin_owner.1) | copy-start | bytes 148
  1.4 1.6 %copy-start.2 = (s32[12]{0:T(128)S(1)}, s32[12]{0:T(128)}, u32[]{:S(2)}) copy-start(s32[12]{0:T(128)} %bin_link.1) | copy-start | bytes 148

commit v4 on v3

--- a/solution.py
+++ b/solution.py
@@ -146,9 +146,9 @@
 
 def owners_kernel(
     n_dp, block, per_bin, rows_dev,
-    feat, weight, row_bin, bin_owner, bin_link,
+    feat3, weight, row_bin, bin_owner, bin_link,
     out_rows, out_weight,
-    wbuf, fcols, fcols_t, outbox, inbox, flag_out, flag_in, grads, returned, gathered,
+    feat, wbuf, fcols, fcols_t, outbox, inbox, flag_out, flag_in, grads, returned, gathered,
     terms, terms16, from_x, pairs, pairs16, from_z,
     w_send, w_recv, f_send, f_recv, flag_send, flag_recv, a_send, a_recv,
     b_send, b_recv, g_send, g_recv, x_send, x_recv, z_send, z_recv,
@@ -202,9 +202,14 @@
         )
         own_w.append((to_sib, to_peer))
 
+    feat[...] = feat3[...].reshape(rows2, feat_dim)
+
     pos = lax.broadcasted_iota(jnp.int32, (rows_dev, rows2), 0)
     lane_row = lax.broadcasted_iota(jnp.int32, (rows_dev, rows2), 1) // 2
-    bin_col = jnp.broadcast_to(row_bin[...], (rows_dev, rows2))
+    spot = lax.broadcasted_iota(jnp.int32, (rows_dev, rows_dev), 0)
+    spot_t = lax.broadcasted_iota(jnp.int32, (rows_dev, rows_dev), 1)
+    bin_col = jnp.sum(jnp.where(spot == spot_t, row_bin[...], 0), axis=1, keepdims=True)
+    bin_col = jnp.broadcast_to(bin_col, (rows_dev, rows2))
     bin_row = jnp.sum(jnp.where(pos == lane_row, bin_col, 0), axis=0, keepdims=True)
     seat = jnp.sum(
         jnp.where((bin_col == bin_row) & (pos < lane_row), 1, 0), axis=0, keepdims=True
@@ -318,17 +323,28 @@
     scale1 = lax.rsqrt(square[1] + 1e-06)
     scale1_row = jnp.sum(jnp.where(eye, scale1, 0.0), axis=0, keepdims=True)
     warm_row = scale1_row * (1.0 / SOFTMAX_TEMP_SCALE)
-    scores = raw * scale0 * warm_row
-    weights = allowed * jnp.exp(scores)
-    shares = weights / jnp.sum(weights, axis=1, keepdims=True)
-    logit = ((shares - jnp.where(eye, 1.0, 0.0)) * valid).astype(BF16).astype(F32)
-    slope = logit * scores
-    lean0 = jnp.sum(slope, axis=1, keepdims=True) * scale0 * scale0
-    lean1_row = jnp.sum(slope, axis=0, keepdims=True) * scale1_row * scale1_row
+    highs, lows, leans = [], [], []
+    lean1_row = jnp.zeros((1, slots), F32)
+    for m in range(n_dp):
+        strip = slice(m * block, (m + 1) * block)
+        score = raw[strip] * scale0[strip] * warm_row
+        weights = allowed[strip] * jnp.exp(score)
+        shares = weights * (1.0 / jnp.sum(weights, axis=1, keepdims=True))
+        same = (
+            lax.broadcasted_iota(jnp.int32, (block, slots), 0) + m * block
+            == lax.broadcasted_iota(jnp.int32, (block, slots), 1)
+        )
+        logit = ((shares - jnp.where(same, 1.0, 0.0)) * valid[strip]).astype(BF16).astype(F32)
+        slope = logit * score
+        leans.append(jnp.sum(slope, axis=1, keepdims=True) * scale0[strip] * scale0[strip])
+        lean1_row += jnp.sum(slope, axis=0, keepdims=True)
+        mix = logit * scale0[strip] * warm_row
+        highs.append(mix.astype(BF16))
+        lows.append((mix - highs[-1].astype(F32)).astype(BF16))
+    lean0 = jnp.concatenate(leans, axis=0)
+    lean1_row = lean1_row * scale1_row * scale1_row
     lean1 = jnp.sum(jnp.where(eye, lean1_row, 0.0), axis=1, keepdims=True)
-    mix = logit * scale0 * warm_row
-    high = mix.astype(BF16)
-    low = (mix - high.astype(F32)).astype(BF16)
+    high, low = jnp.concatenate(highs, axis=0), jnp.concatenate(lows, axis=0)
     high_t, low_t = high.T, low.T
 
     back_copies = []
@@ -435,6 +451,7 @@
         in_specs=[vmem, vmem, vmem, smem, smem],
         out_specs=(vmem, vmem),
         scratch_shapes=[
+            pltpu.VMEM((rows2, feat_dim), BF16),
             pltpu.VMEM((3, part, emb), BF16),
             pltpu.VMEM((4 * rows2, part), BF16),
             pltpu.VMEM((part, 4 * rows2), BF16),
@@ -464,7 +481,7 @@
         cost_estimate=pl.CostEstimate(
             flops=4 * rows2 * feat_dim * emb, bytes_accessed=16 * 1024 * 1024, transcendentals=0
         ),
-    )(features.reshape(rows2, feat_dim), head_weight, bin_of_row, bin_owner, bin_link)
+    )(features, head_weight, bin_of_row.reshape(1, rows_dev), bin_owner, bin_link)
     return grad_rows.reshape(rows_dev, views, emb), grad_weight
 
 

time: 116 us -> 116 us (level)
    unnamed x8 -> x11, local copies, waits for them, and re-layouts: 1.48 us -> 3.81 us
    reshape x1 -> x0, local copies, waits for them, and re-layouts: 1.55 us -> none  [local_kernel(): features.reshape(rows2, feat_dim)]
where the time goes in v4:
time: 116 us
  Pallas kernels  110 us (95%)
  local copies, waits for them, and re-layouts  4.81 us (4%)
    pallas_call x1, Pallas kernels, local_kernel(): pl.pallas_call(functools.partial(owners_kernel, n_dp, block, per_bin, row...  110 us
    unnamed x11, local copies, waits for them, and re-layouts  3.81 us

profile of v4, /device:TPU:0, one launch (start us, length us, event | category | flops | bytes accessed | tf_op | source)
XLA Modules:
  0.0 115.9 jit_solution(5195780294977098590)
XLA Ops:
  0.6 0.0 copy-start.4
  0.6 0.0 copy-start.3
  0.7 0.0 copy-start.2
  0.7 0.6 copy-done.4
  1.3 0.0 copy-done.3
  1.3 0.0 copy-done.2
  1.3 0.0 copy-start
  1.3 1.2 %copy-done = bf16[128,2,2048]{2,1,0:T(2,128)(2,1)S(1)} copy-done((bf16[128,2,2048]{2,1,0:T(2,128)(2,1)S(1)}, bf16[128,2,2048]{2,1,0:T(2,128)(2,1)}, u32[]{:S(2)}) %copy-start) | copy-done | bytes 1048600
  2.5 0.0 copy-start.1
  2.5 1.2 %copy-done.1 = bf16[512,1024]{1,0:T(8,128)(2,1)S(1)} copy-done((bf16[512,1024]{1,0:T(8,128)(2,1)S(1)}, bf16[512,1024]{1,0:T(8,128)(2,1)}, u32[]{:S(2)}) %copy-start.1) | copy-done | bytes 1048600
  3.8 110.4 %shard_map.68 = (bf16[256,1024]{1,0:T(8,128)(2,1)S(1)}, f32[64,1024]{1,0:T(8,128)S(1)}) custom-call(bf16[128,2,2048]{2,1,0:T(2,128)(2,1)S(1)} %copy-done, bf16[512,1024]{1,0:T(8,128)(2,1)S(1)} %copy-done.1, s32[1,128]{1,0:T(1,128)S(1)} %bitcast.1, s32[12]{0:T(128)S(1)} %copy-done.3, s32[12]{0:T(128)S(1)} %copy-done.4), custom_call_target="tpu_custom_call" | custom-call | flops 2147483648 | bytes 16777216 | tf_op jit(solution)/shard_map/pallas_call | solution.py:445
  114.2 1.0 reshape.11
  115.2 0.7 copy.8
Async XLA Ops:
  0.6 0.7 copy-start.4
  0.6 0.7 copy-start.3
  0.7 0.7 copy-start.2
  1.3 1.2 %copy-start = (bf16[128,2,2048]{2,1,0:T(2,128)(2,1)S(1)}, bf16[128,2,2048]{2,1,0:T(2,128)(2,1)}, u32[]{:S(2)}) copy-start(bf16[128,2,2048]{2,1,0:T(2,128)(2,1)} %feat3.1) | copy-start | bytes 3145732
  2.5 1.2 %copy-start.1 = (bf16[512,1024]{1,0:T(8,128)(2,1)S(1)}, bf16[512,1024]{1,0:T(8,128)(2,1)}, u32[]{:S(2)}) copy-start(bf16[512,1024]{1,0:T(8,128)(2,1)} %weight.1) | copy-start | bytes 3145732

commit v5 on v4

--- a/solution.py
+++ b/solution.py
@@ -193,11 +193,11 @@
     own_w = []
     for k in range(CHUNKS):
         to_peer = push(
-            weight.at[:, lanes[k]], wbuf.at[1, :, lanes[k]],
+            weight.at[:, lanes[k]], wbuf[k].at[1],
             w_send.at[1, k], w_recv.at[1, k], (dp, peer),
         )
         to_sib = push(
-            weight.at[:, lanes[k]], wbuf.at[0, :, lanes[k]],
+            weight.at[:, lanes[k]], wbuf[k].at[0],
             w_send.at[0, k], w_recv.at[0, k], (dp, sib),
         )
         own_w.append((to_sib, to_peer))
@@ -248,7 +248,7 @@
         def block_copy(m):
             span = pl.ds(pl.multiple_of(m * block, block), block)
             return pltpu.make_async_remote_copy(
-                src_ref=src.at[:, span, lanes[k]], dst_ref=dst.at[:, span, lanes[k]],
+                src_ref=src[k].at[:, span, :], dst_ref=dst[k].at[:, span, :],
                 send_sem=send.at[k, m], recv_sem=recv.at[k, m],
                 device_id=(mixed(dp, m, n_dp), col), device_id_type=MESH,
             )
@@ -267,20 +267,20 @@
         to_sib, to_peer = own_w[k]
         to_peer.wait_recv()
         relay = push(
-            wbuf.at[1, :, lanes[k]], wbuf.at[2, :, lanes[k]],
+            wbuf[k].at[1], wbuf[k].at[2],
             w_send.at[2, k], w_recv.at[2, k], (dp, sib),
         )
         y = jnp.dot(feat[:, columns_of(col)], weight[:, lanes[k]], preferred_element_type=F32)
-        y += jnp.dot(feat[:, columns_of(peer)], wbuf[1, :, lanes[k]], preferred_element_type=F32)
+        y += jnp.dot(feat[:, columns_of(peer)], wbuf[k][1], preferred_element_type=F32)
         to_sib.wait_recv()
-        y += jnp.dot(feat[:, columns_of(sib)], wbuf[0, :, lanes[k]], preferred_element_type=F32)
+        y += jnp.dot(feat[:, columns_of(sib)], wbuf[k][0], preferred_element_type=F32)
         relay.wait_recv()
-        y += jnp.dot(feat[:, columns_of(diag)], wbuf[2, :, lanes[k]], preferred_element_type=F32)
+        y += jnp.dot(feat[:, columns_of(diag)], wbuf[k][2], preferred_element_type=F32)
         y = y.astype(BF16)
         for v in range(2):
             placed = jnp.dot(pick[v], y, preferred_element_type=F32).astype(BF16)
-            outbox[v, :, lanes[k]] = placed
-            inbox[v, 0:block, lanes[k]] = placed[0:block]
+            outbox[k][v] = placed
+            inbox[k][v, 0:block, :] = placed[0:block]
         out_copies.append(exchange(outbox, inbox, a_send, a_recv, k))
 
     f_copies = []
@@ -314,10 +314,10 @@
         for copy in out_copies[k]:
             copy.wait_recv()
         raw += lax.dot_general(
-            inbox[0, :, lanes[k]], inbox[1, :, lanes[k]], (((1,), (1,)), ((), ())), preferred_element_type=F32
+            inbox[k][0], inbox[k][1], (((1,), (1,)), ((), ())), preferred_element_type=F32
         )
         for v in range(2):
-            row = inbox[v, :, lanes[k]].astype(F32)
+            row = inbox[k][v].astype(F32)
             square[v] += jnp.sum(row * row, axis=1, keepdims=True)
     scale0 = lax.rsqrt(square[0] + 1e-06)
     scale1 = lax.rsqrt(square[1] + 1e-06)
@@ -349,14 +349,14 @@
 
     back_copies = []
     for k in range(CHUNKS):
-        y0, y1 = inbox[0, :, lanes[k]], inbox[1, :, lanes[k]]
+        y0, y1 = inbox[k][0], inbox[k][1]
         g0 = jnp.dot(high, y1, preferred_element_type=F32)
         g0 += jnp.dot(low, y1, preferred_element_type=F32) - lean0 * y0.astype(F32)
         g1 = jnp.dot(high_t, y0, preferred_element_type=F32)
         g1 += jnp.dot(low_t, y0, preferred_element_type=F32) - lean1 * y1.astype(F32)
         for v, g in ((0, g0.astype(BF16)), (1, g1.astype(BF16))):
-            grads[v, :, lanes[k]] = g
-            returned[v, 0:block, lanes[k]] = g[0:block]
+            grads[k][v] = g
+            returned[k][v, 0:block, :] = g[0:block]
         back_copies.append(exchange(grads, returned, b_send, b_recv, k))
 
     for x, copy in zip((2, 3, 1), f_copies):
@@ -369,14 +369,14 @@
 
     def finish_pair(k):
         x_copies[k].wait_recv()
-        pair = terms[:, side, :, lanes[k]] + from_x[:, :, lanes[k]].astype(F32)
+        pair = terms[:, side, :, lanes[k]] + from_x[k][...].astype(F32)
         pairs[:, :, lanes[k]] = pair
-        pairs16[:, :, lanes[k]] = pair.astype(BF16)
+        pairs16[k][...] = pair.astype(BF16)
         copies = []
         for step in range(layers - 1, 0, -1):
             to = lax.rem(layer + step, layers)
             copies.append(push(
-                pairs16.at[to, :, lanes[k]], from_z.at[step, :, lanes[k]],
+                pairs16[k].at[to], from_z[k].at[step],
                 z_send.at[k, step], z_recv.at[k, step], (to * 2 + side, col),
             ))
         z_copies.append(copies)
@@ -386,33 +386,33 @@
             copy.wait_recv()
         rows = jnp.zeros((rows2, WIDTHS[k]), F32)
         for v in range(2):
-            rows += jnp.dot(pick_t[v], returned[v, :, lanes[k]], preferred_element_type=F32)
+            rows += jnp.dot(pick_t[v], returned[k][v], preferred_element_type=F32)
         rows = rows.astype(BF16)
         out_rows[:, lanes[k]] = rows
-        gathered[0:rows2, lanes[k]] = rows
-        own = gathered.at[pl.ds(0, rows2), lanes[k]]
+        gathered[k][0:rows2, :] = rows
+        own = gathered[k].at[pl.ds(0, rows2), :]
         spans = [pl.ds(x * rows2, rows2) for x in range(4)]
         to_peer = push(
-            own, gathered.at[spans[2], lanes[k]], g_send.at[1, k], g_recv.at[1, k], (dp, peer)
+            own, gathered[k].at[spans[2], :], g_send.at[1, k], g_recv.at[1, k], (dp, peer)
         )
         to_sib = push(
-            own, gathered.at[spans[1], lanes[k]], g_send.at[0, k], g_recv.at[0, k], (dp, sib)
+            own, gathered[k].at[spans[1], :], g_send.at[0, k], g_recv.at[0, k], (dp, sib)
         )
         if k > 0:
             finish_pair(k - 1)
         to_peer.wait_recv()
         relay = push(
-            gathered.at[spans[2], lanes[k]], gathered.at[spans[3], lanes[k]],
+            gathered[k].at[spans[2], :], gathered[k].at[spans[3], :],
             g_send.at[2, k], g_recv.at[2, k], (dp, sib),
         )
         to_sib.wait_recv()
         relay.wait_recv()
-        term = jnp.dot(fcols_t[...], gathered[:, lanes[k]], preferred_element_type=F32)
+        term = jnp.dot(fcols_t[...], gathered[k][...], preferred_element_type=F32)
         term = term.reshape(layers, 2, piece, WIDTHS[k])
         terms[:, :, :, lanes[k]] = term
-        terms16[:, :, :, lanes[k]] = term.astype(BF16)
+        terms16[k][...] = term.astype(BF16)
         x_copies.append(push(
-            terms16.at[:, 1 - side, :, lanes[k]], from_x.at[:, :, lanes[k]],
+            terms16[k].at[:, 1 - side], from_x[k],
             x_send.at[k], x_recv.at[k], (across, col),
         ))
     finish_pair(CHUNKS - 1)
@@ -421,7 +421,7 @@
         for copy in z_copies[k]:
             copy.wait_recv()
         for step in range(1, layers):
-            total += from_z[step, :, lanes[k]].astype(F32)
+            total += from_z[k][step].astype(F32)
         out_weight[:, lanes[k]] = total / rows_dev
     for copy in sends:
         copy.wait_send()
@@ -441,7 +441,11 @@
     vmem = pl.BlockSpec(memory_space=pltpu.VMEM)
     smem = pl.BlockSpec(memory_space=pltpu.SMEM)
     dma = pltpu.SemaphoreType.DMA
-    wide = pltpu.VMEM((views, slots, emb), BF16)
+
+    def chunked(*shape):
+        return tuple(pltpu.VMEM((*shape, width), BF16) for width in WIDTHS)
+
+    wide = chunked(views, slots)
     grad_rows, grad_weight = pl.pallas_call(
         functools.partial(owners_kernel, n_dp, block, per_bin, rows_dev),
         out_shape=(
@@ -452,20 +456,20 @@
         out_specs=(vmem, vmem),
         scratch_shapes=[
             pltpu.VMEM((rows2, feat_dim), BF16),
-            pltpu.VMEM((3, part, emb), BF16),
+            chunked(3, part),
             pltpu.VMEM((4 * rows2, part), BF16),
             pltpu.VMEM((part, 4 * rows2), BF16),
             wide, wide,
             pltpu.VMEM((slots, 128), BF16),
             pltpu.VMEM((slots, 128), BF16),
             wide, wide,
-            pltpu.VMEM((4 * rows2, emb), BF16),
+            chunked(4 * rows2),
             pltpu.VMEM((layers, 2, piece, emb), F32),
-            pltpu.VMEM((layers, 2, piece, emb), BF16),
-            pltpu.VMEM((layers, piece, emb), BF16),
+            chunked(layers, 2, piece),
+            chunked(layers, piece),
             pltpu.VMEM((layers, piece, emb), F32),
-            pltpu.VMEM((layers, piece, emb), BF16),
-            pltpu.VMEM((layers, piece, emb), BF16),
+            chunked(layers, piece),
+            chunked(layers, piece),
             dma((3, CHUNKS)), dma((3, CHUNKS)),
             dma((4,)), dma((4,)),
             dma((n_dp,)), dma((n_dp,)),

time: 116 us -> 116 us (level)
  no operation moved by 1% of the time
where the time goes in v5:
time: 116 us
  Pallas kernels  110 us (95%)
  local copies, waits for them, and re-layouts  4.81 us (4%)
    pallas_call x1, Pallas kernels, local_kernel(): pl.pallas_call(functools.partial(owners_kernel, n_dp, block, per_bin, row...  110 us
    unnamed x11, local copies, waits for them, and re-layouts  3.81 us

profile of v5, /device:TPU:0, one launch (start us, length us, event | category | flops | bytes accessed | tf_op | source)
XLA Modules:
  0.0 115.9 jit_solution(15336429652427384388)
XLA Ops:
  0.6 0.0 copy-start.4
  0.6 0.0 copy-start.3
  0.7 0.0 copy-start.2
  0.7 0.6 copy-done.4
  1.3 0.0 copy-done.3
  1.3 0.0 copy-done.2
  1.3 0.0 copy-start
  1.3 1.2 %copy-done = bf16[128,2,2048]{2,1,0:T(2,128)(2,1)S(1)} copy-done((bf16[128,2,2048]{2,1,0:T(2,128)(2,1)S(1)}, bf16[128,2,2048]{2,1,0:T(2,128)(2,1)}, u32[]{:S(2)}) %copy-start) | copy-done | bytes 1048600
  2.5 0.0 copy-start.1
  2.5 1.2 %copy-done.1 = bf16[512,1024]{1,0:T(8,128)(2,1)S(1)} copy-done((bf16[512,1024]{1,0:T(8,128)(2,1)S(1)}, bf16[512,1024]{1,0:T(8,128)(2,1)}, u32[]{:S(2)}) %copy-start.1) | copy-done | bytes 1048600
  3.8 110.5 %shard_map.68 = (bf16[256,1024]{1,0:T(8,128)(2,1)S(1)}, f32[64,1024]{1,0:T(8,128)S(1)}) custom-call(bf16[128,2,2048]{2,1,0:T(2,128)(2,1)S(1)} %copy-done, bf16[512,1024]{1,0:T(8,128)(2,1)S(1)} %copy-done.1, s32[1,128]{1,0:T(1,128)S(1)} %bitcast.1, s32[12]{0:T(128)S(1)} %copy-done.3, s32[12]{0:T(128)S(1)} %copy-done.4), custom_call_target="tpu_custom_call" | custom-call | flops 2147483648 | bytes 16777216 | tf_op jit(solution)/shard_map/pallas_call | solution.py:449
  114.3 1.0 reshape.11
  115.2 0.7 copy.8
Async XLA Ops:
  0.6 0.7 copy-start.4
  0.6 0.7 copy-start.3
  0.7 0.7 copy-start.2
  1.3 1.2 %copy-start = (bf16[128,2,2048]{2,1,0:T(2,128)(2,1)S(1)}, bf16[128,2,2048]{2,1,0:T(2,128)(2,1)}, u32[]{:S(2)}) copy-start(bf16[128,2,2048]{2,1,0:T(2,128)(2,1)} %feat3.1) | copy-start | bytes 3145732
  2.5 1.2 %copy-start.1 = (bf16[512,1024]{1,0:T(8,128)(2,1)S(1)}, bf16[512,1024]{1,0:T(8,128)(2,1)}, u32[]{:S(2)}) copy-start(bf16[512,1024]{1,0:T(8,128)(2,1)} %weight.1) | copy-start | bytes 3145732
